TPU v7x, 32 devices: a whole 2x2x4 slice. The times are simulated.
32 devices in a mesh: section: 2 (over core), dp: 4 (over y, x), seq: 4 (over z).
Axes of the slice: x: 2, y: 2, z: 4, core: 2. Of those that a mesh axis runs over, the one named last changes fastest.
Arguments:
- tokens: bfloat16 [16, 1024, 512], P('dp', 'seq'), may hold values from -6 to 6
- cotangent: bfloat16 [16, 1024, 512], P('dp', 'seq'), may hold values from -6 to 6
- tap_masks: int32 [2, 9, 16, 1024], P('section', None, 'dp', 'seq'), may hold values from 0 to 1, as said below
- conv_weight: bfloat16 [2, 512, 9, 512], P('section'), may hold values from -0.09375 to 0.09375
- up_weight: bfloat16 [2, 512, 2048], P('section'), may hold values from -0.25 to 0.25
- up_bias: float32 [2, 2048], P('section'), may hold values from -1.5 to 1.5
- down_weight: bfloat16 [2, 2048, 512], P('section'), may hold values from -0.125 to 0.125
- norm_gains: float32 [2, 512, 2], P('section'), may hold values from 0.25 to 1.75
- shift_terms: float32 [2, 512, 4], P('section'), may hold values from -1.5 to 1.5
Outputs:
- activations: bfloat16 [2, 16, 1024, 512], P('section', 'dp', 'seq')
- in_grads: float32 [2, 16, 1024, 512], P('section', 'dp', 'seq')
- conv_grad: float32 [2, 512, 9, 512], P('section', ('dp', 'seq'))
- up_grad: float32 [2, 512, 2048], P('section', ('dp', 'seq'))
- up_bias_grad: float32 [2, 2048], P('section', ('dp', 'seq'))
- down_grad: float32 [2, 2048, 512], P('section', ('dp', 'seq'))
- gain_grad: float32 [2, 512, 2], P('section', ('dp', 'seq'))
- shift_grad: float32 [2, 512, 4], P('section', ('dp', 'seq'))
Inputs may be any that keep to these rules, and one draw needn't show every extreme that they name: tap_masks[s, k, r, p] is 1 exactly when position p + (k - 4) * d of row r lies inside the row and in the same contig (a run of positions) as p, with d = 2 for s = 0 and 32 for s = 1.
All inputs are finite; a program needn't handle non-finite values.
Results may differ from a plain program's by a relative error of at most 0.0095.
Values may be sent and summed in bfloat16 or wider, within the bound.
A program may use at most 192 MiB of HBM per device.

v0:
```python
import functools

import jax
import jax.numpy as jnp
from jax import lax
from jax.experimental import pallas as pl
from jax.experimental.pallas import tpu as pltpu
from jax.sharding import PartitionSpec as P

TAPS = 9
CENTRE = TAPS // 2
TIGHT = 2
WIDE = 32
HALO = CENTRE * WIDE
EDGE = 16
EPS = 1e-05
MESH = pl.DeviceIdType.MESH
BF16 = jnp.bfloat16
F32 = jnp.float32
LAG = 3
FIRST_GROUPS = 2
PLAN = (
    ("conv", 4), ("conv", 3), ("conv", 1), (8, 0), ("other", 0), ("up", 1), (7, 0), (8, 1), ("conv", 0), (5, 0),
    ("first", 0), ("conv", 2), ("down", 0), (8, 2), ("up", 0), (4, 0), (7, 1), ("down", 1), (1, 0), (0, 0), (4, 1),
    (6, 0), (7, 2), (5, 1), (2, 0), (1, 1), (3, 0), (6, 1), (5, 2), (0, 1), ("first", 1), (5, 3), (7, 3), (4, 2),
    (3, 1), (2, 1), (6, 2), (1, 2), (8, 3), (0, 2), (3, 2), (6, 3), (4, 3), (1, 3), (0, 3), (2, 2),
)
ALONG = (5, 7, 8)
TANH_SCALE = 0.7978845608028654
TANH_CUBE = TANH_SCALE * 0.044715


def gelu_pair(z):
    square = z * z
    half = 0.5 + 0.5 * jnp.tanh(z * (TANH_SCALE + TANH_CUBE * square))
    value = z * half
    return value, half + value * (1.0 - half) * (2.0 * TANH_SCALE + 6.0 * TANH_CUBE * square)


def normalise(values):
    centred = values - jnp.mean(values, axis=-1, keepdims=True)
    scale = lax.rsqrt(jnp.mean(centred * centred, axis=-1, keepdims=True) + EPS)
    return centred * scale, scale


def norm_backward(weighted, unit):
    return (
        weighted
        - jnp.mean(weighted, axis=-1, keepdims=True)
        - unit * jnp.mean(weighted * unit, axis=-1, keepdims=True)
    )


def column_sum(values):
    return jnp.sum(values, axis=0, keepdims=True)


def dot(a, b):
    return jnp.dot(a, b, preferred_element_type=F32)


def dot_nt(a, b):
    return lax.dot_general(a, b, (((1,), (1,)), ((), ())), preferred_element_type=F32)


def dot_tn(a, b):
    return lax.dot_general(a, b, (((0,), (0,)), ((), ())), preferred_element_type=F32)


class Geometry:
    def __init__(self, dp, seq, rows, length, width, hidden):
        self.dp, self.seq = dp, seq
        self.rows, self.length, self.width = rows, length, width
        self.tokens = rows * length
        self.chunks = hidden // width
        self.low = max(1, 16 * dp * seq // width)
        self.owners = dp * seq // self.low
        self.share = width // self.owners
        self.final_share = width // (dp * seq)
        self.bias_share = hidden // (dp * seq)
        dp_bits = [("dp", 1 << i) for i in range(dp.bit_length() - 1)]
        seq_all = [("seq", 1 << i) for i in range(seq.bit_length() - 1)]
        seq_bits = [bit for bit in seq_all if bit[1] >= self.low]
        self.bits = dp_bits + seq_bits
        self.all_bits = dp_bits + seq_all
        self.dp_bits = dp_bits
        self.pairs = (TAPS + 1) // 2
        self.part_chunks = self.chunks // 2
        self.slices = 2 * self.part_chunks + self.pairs
        low_bit, high_bit, lines = dp_bits[:1], dp_bits[-1:], seq_bits
        self.orders = [low_bit + lines + high_bit] * self.part_chunks + [low_bit + lines] * self.part_chunks
        self.orders += [high_bit + lines + low_bit] * self.pairs
        for j in range(self.slices):
            if j in ALONG:
                self.orders[j] = lines[:1] + self.orders[j][:1] + self.orders[j][2:]
        planned = len(self.bits) == 4 and rows == 4 and self.chunks == 4
        self.plan = PLAN if planned else self.plain_plan()

    def plain_plan(self):
        first_down, first_conv = self.part_chunks, 2 * self.part_chunks
        work = [("other", 0)]
        work += [("down", i) for i in range(self.part_chunks)]
        work += [("up", i) for i in range(self.part_chunks)]
        work += [("conv", p) for p in range(self.pairs)]
        work += [("first", group) for group in range(FIRST_GROUPS)]
        due = {}
        for turn, (kind, at) in enumerate(work):
            begun = {"up": [at], "conv": [first_conv + at]}.get(kind, [])
            if kind == "down" and at == self.part_chunks - 1:
                begun = range(first_down, first_conv)
            for j in begun:
                for i in range(len(self.orders[j])):
                    due.setdefault(turn + LAG * (i + 1), []).append((j, i))
        plan = []
        for turn in range(max(max(due) + 1, len(work))):
            plan += work[turn : turn + 1] + due.get(turn, [])
        return plan


def body(
    geo,
    tokens_hbm,
    cotangent_hbm,
    conv_hbm,
    up_hbm,
    down_hbm,
    masks,
    bias,
    gains,
    shifts,
    act_hbm,
    grads_hbm,
    conv_out,
    up_out,
    down_out,
    bias_out,
    gain_out,
    shift_out,
    fields,
    conv_grads,
    near_edges,
    conv_w,
    up_w,
    down_w,
    slabs,
    taps,
    halves,
    unit_one,
    slope_one,
    unit_two,
    scale_two,
    mixed_grads,
    given,
    ffn_grads,
    mixed_other,
    ffn_grads_other,
    upper_other,
    hidden_other,
    results,
    masks_other,
    masks_second,
    columns,
    columns_second,
    conv_total,
    partial,
    arrived,
    sums,
    sums_sent,
    sums_arrived,
    load_sem,
    row_load_sem,
    token_edge_send,
    token_edge_recv,
    masks_send,
    masks_recv,
    pass_send,
    pass_recv,
    field_send,
    field_recv,
    weight_send,
    weight_recv,
    back_send,
    back_recv,
    half_send,
    half_recv,
    mixed_send,
    mixed_recv,
    ffn_send,
    ffn_recv,
    near_send,
    near_recv,
    act_sem,
    grads_sem,
    grads_send,
    grads_recv,
    part_send,
    part_recv,
    sums_send,
    sums_recv,
):
    rows, length, width, chunks = geo.rows, geo.length, geo.width, geo.chunks
    tokens, half_width = geo.tokens, geo.width // 2
    section = lax.axis_index("section")
    dp = lax.axis_index("dp")
    seq = lax.axis_index("seq")
    mine = {"dp": dp, "seq": seq}
    in_first = section == 0
    in_second = section == 1
    has_left = (seq + geo.seq - 1) // geo.seq
    has_right = 1 - (seq + 1) // geo.seq
    on_left, on_right = has_left == 1, has_right == 1
    own = slice(HALO, HALO + length)
    near = slice(HALO - EDGE, HALO + length + EDGE)

    def bit_of(bit):
        axis, size = bit
        return (mine[axis] // size) % 2

    def partner(bit):
        axis, size = bit
        other = mine[axis] + (1 - 2 * bit_of(bit)) * size
        return (section, other, seq) if axis == "dp" else (section, dp, other)

    def remote(source, target, sends, receives, device):
        return pltpu.make_async_remote_copy(
            src_ref=source,
            dst_ref=target,
            send_sem=sends,
            recv_sem=receives,
            device_id=device,
            device_id_type=MESH,
        )

    core = (1 - section, dp, seq)
    left, right = (section, dp, seq - 1), (section, dp, seq + 1)
    first_core, second_core = (0, dp, seq), (1, dp, seq)
    conv_bit, ffn_bit = geo.dp_bits[0], geo.dp_bits[-1]
    pair, ffn_pair = partner(conv_bit), partner(ffn_bit)
    my_half, my_part = bit_of(conv_bit), bit_of(ffn_bit)
    part_chunks = geo.part_chunks
    mine_at = pl.ds(pl.multiple_of(my_half * half_width, half_width), half_width)
    other_at = pl.ds(pl.multiple_of((1 - my_half) * half_width, half_width), half_width)

    loads = [
        pltpu.make_async_copy(conv_hbm, conv_w, load_sem.at[0]),
        pltpu.make_async_copy(up_hbm, up_w, load_sem.at[1]),
        pltpu.make_async_copy(down_hbm, down_w, load_sem.at[2]),
    ]
    token_load = pltpu.make_async_copy(tokens_hbm, fields.at[0:rows, own], row_load_sem.at[0])
    given_load = pltpu.make_async_copy(cotangent_hbm, given, row_load_sem.at[1])
    pl.when(in_first)(token_load.start)
    for load in loads:
        load.start()
    pl.when(in_second)(given_load.start)

    @pl.when(has_left == 0)
    def _():
        fields[0:rows, :HALO] = jnp.zeros((rows, HALO, width), BF16)
        conv_grads[:, :HALO] = jnp.zeros((rows, HALO, width), BF16)

    @pl.when(has_right == 0)
    def _():
        fields[0:rows, HALO + length :] = jnp.zeros((rows, HALO, width), BF16)
        conv_grads[:, HALO + length :] = jnp.zeros((rows, HALO, width), BF16)

    sums[...] = jnp.zeros(sums.shape, F32)

    barrier = pltpu.get_barrier_semaphore()

    def greet(device):
        pl.semaphore_signal(barrier, inc=1, device_id=device, device_id_type=MESH)

    for bit in geo.all_bits:
        greet(partner(bit))
    greet(core)
    for flag, at in ((on_left, seq - 1), (on_right, seq + 1)):

        @pl.when(flag)
        def _(at=at):
            greet((section, dp, at))
            greet((1 - section, dp, at))

    pl.semaphore_wait(barrier, len(geo.all_bits) + 1 + 2 * has_left + 2 * has_right)

    tokens_right = remote(
        tokens_hbm.at[:, length - EDGE : length],
        fields.at[0:rows, HALO - EDGE : HALO],
        token_edge_send.at[0],
        token_edge_recv.at[0],
        right,
    )
    tokens_left = remote(
        tokens_hbm.at[:, 0:EDGE],
        fields.at[0:rows, HALO + length : HALO + length + EDGE],
        token_edge_send.at[1],
        token_edge_recv.at[1],
        left,
    )

    @pl.when(in_first)
    def _():
        pl.when(on_right)(tokens_right.start)
        pl.when(on_left)(tokens_left.start)

    masks_across = remote(masks, masks_other, masks_send.at[0], masks_recv.at[0], pair)
    masks_back = remote(masks, masks_second, masks_send.at[1], masks_recv.at[1], first_core)
    masks_across.start()
    pl.when(in_second)(masks_back.start)

    def to_columns(source, target, base=0):
        for r in range(rows):
            plane = source[:, r, :].astype(F32)
            padded = jnp.concatenate([plane, jnp.zeros((128 - TAPS, length), F32)], axis=0)
            target[base + r * length : base + (r + 1) * length, :] = jnp.transpose(padded)

    to_columns(masks, columns)

    def span(m):
        return pl.ds(pl.multiple_of(m * length, length), length)

    def one_tap(source, mask_columns, m, k, dilation):
        values = source[m, pl.ds(HALO + (k - CENTRE) * dilation, length), :]
        if k == CENTRE:
            return values
        lane = jnp.broadcast_to(mask_columns[span(m), k : k + 1], (length, 128)).astype(BF16)
        return values * jnp.concatenate([lane] * (width // 128), axis=1)

    def pass_copies(m):
        return (
            remote(results.at[m], fields.at[m, own], pass_send.at[m, 0], pass_recv.at[m, 0], second_core),
            remote(
                results.at[m, length - HALO : length],
                fields.at[m, 0:HALO],
                pass_send.at[m, 1],
                pass_recv.at[m, 1],
                (1, dp, seq + 1),
            ),
            remote(
                results.at[m, 0:HALO],
                fields.at[m, HALO + length : HALO + length + HALO],
                pass_send.at[m, 2],
                pass_recv.at[m, 2],
                (1, dp, seq - 1),
            ),
        )

    def back_copies(m):
        return (
            remote(conv_grads.at[m, own], conv_grads.at[m, own], back_send.at[m, 0], back_recv.at[m, 0], first_core),
            remote(mixed_grads.at[m], mixed_grads.at[m], back_send.at[m, 1], back_recv.at[m, 1], first_core),
            remote(
                conv_grads.at[m, HALO + length - HALO : HALO + length],
                conv_grads.at[m, 0:HALO],
                back_send.at[m, 2],
                back_recv.at[m, 2],
                (0, dp, seq + 1),
            ),
            remote(
                conv_grads.at[m, HALO : HALO + HALO],
                conv_grads.at[m, HALO + length : HALO + length + HALO],
                back_send.at[m, 3],
                back_recv.at[m, 3],
                (0, dp, seq - 1),
            ),
        )

    def near_copies(m):
        return (
            remote(
                conv_grads.at[m, HALO + length - EDGE : HALO + length],
                near_edges.at[m, 0],
                near_send.at[m, 0],
                near_recv.at[m, 0],
                right,
            ),
            remote(
                conv_grads.at[m, HALO : HALO + EDGE],
                near_edges.at[m, 1],
                near_send.at[m, 1],
                near_recv.at[m, 1],
                left,
            ),
        )

    def field_copy(m):
        return remote(fields.at[m], fields.at[rows + m], field_send.at[m], field_recv.at[m], pair)

    near_fields = remote(
        fields.at[0:rows, near], fields.at[rows : 2 * rows, near], field_send.at[0], field_recv.at[0], pair
    )

    def half_copy(m):
        return remote(
            conv_grads.at[m, own, other_at],
            halves.at[pl.ds(pl.multiple_of(tokens + m * length, length), length)],
            half_send.at[m],
            half_recv.at[m],
            pair,
        )

    def mixed_copy(m):
        here = span(m)
        return remote(
            slabs.at[2 * chunks, here], mixed_other.at[here], mixed_send.at[m], mixed_recv.at[m], ffn_pair
        )

    def ffn_copy(m):
        here = span(m)
        return remote(ffn_grads.at[here], ffn_grads_other.at[here], ffn_send.at[m], ffn_recv.at[m], ffn_pair)

    weight_copy = remote(conv_w, conv_w, weight_send, weight_recv, first_core)

    def act_copy(m):
        return pltpu.make_async_copy(results.at[m], act_hbm.at[m], act_sem.at[m])

    def grads_copy(m):
        return pltpu.make_async_copy(mixed_grads.at[m], grads_hbm.at[m], grads_sem.at[m])

    def grads_across(m):
        return remote(mixed_grads.at[m], grads_hbm.at[m], grads_send.at[m], grads_recv.at[m], second_core)

    for load in loads:
        load.wait()

    @pl.when(in_first)
    def _():
        token_load.wait()
        pl.when(on_left)(tokens_right.wait_recv)
        pl.when(on_right)(tokens_left.wait_recv)
        near_fields.start()

    gain_one, gain_two = gains[0:1, :], gains[1:2, :]
    shift_conv, shift_one = shifts[0:1, :], shifts[1:2, :]
    shift_ffn, shift_two = shifts[2:3, :], shifts[3:4, :]

    def forward(m, carry):
        here = span(m)

        @pl.when(in_second)
        def _():
            whole, low, high = pass_copies(m)
            whole.wait_recv()
            pl.when(on_left)(low.wait_recv)
            pl.when(on_right)(high.wait_recv)
            field_copy(m).start()
            pl.when(m == rows - 1)(weight_copy.start)

        for flag, dilation in ((in_first, TIGHT), (in_second, WIDE)):

            @pl.when(flag)
            def _(dilation=dilation):
                for k in range(TAPS):
                    taps[:, k * width : (k + 1) * width] = one_tap(fields, columns, m, k, dilation)

        value, slope = gelu_pair(dot(taps[...], conv_w[...]) + shift_conv)
        unit, scale = normalise(value)
        unit_one[here, :] = unit.astype(BF16)
        slope_one[here, :] = (slope * scale).astype(BF16)
        mixed = fields[m, own, :].astype(F32) + unit * gain_one + shift_one
        mixed_low = mixed.astype(BF16)
        slabs[2 * chunks, here, :] = mixed_low
        mixed_copy(m).start()
        ffn = None
        for c in range(chunks):
            part = slice(c * width, (c + 1) * width)
            value, slope = gelu_pair(dot(mixed_low, up_w[:, part]) + bias[:, part])
            low = value.astype(BF16)
            slabs[c, here, :] = low
            slabs[chunks + c, here, :] = slope.astype(BF16)
            term = dot(low, down_w[part, :])
            ffn = term if ffn is None else ffn + term
        unit, scale = normalise(ffn + shift_ffn)
        unit_two[here, :] = unit.astype(BF16)
        scale_two[here, :] = jnp.broadcast_to(scale, (length, 128))
        results[m] = (mixed + unit * gain_two + shift_two).astype(BF16)
        act_copy(m).start()

        @pl.when(in_first)
        def _():
            whole, low, high = pass_copies(m)
            pl.when(on_right)(low.start)
            pl.when(on_left)(high.start)
            whole.start()

        return carry

    lax.fori_loop(0, rows, forward, 0)

    masks_across.wait_recv()
    to_columns(masks_other, columns, tokens)

    @pl.when(in_first)
    def _():
        masks_back.wait_recv()
        to_columns(masks_second, columns_second)

    def conv_back(m, mask_columns, dilation):
        grad = mixed_grads[m]
        for k in range(TAPS):
            at = (TAPS - 1 - k) * width
            grad = grad + dot_nt(one_tap(conv_grads, mask_columns, m, k, dilation), conv_w[at : at + width, :])
        return grad

    def chunk_of(i):
        return my_part * part_chunks + i

    def chunk_span(i):
        return pl.ds(pl.multiple_of(chunk_of(i) * width, width), width)

    def other_forward(m, carry):
        here = span(m)
        mixed_copy(m).wait_recv()
        for i in range(part_chunks):
            at = chunk_span(i)
            value, slope = gelu_pair(dot(mixed_other[here, :], up_w[:, at]) + bias[:, at])
            upper_other[i, here, :] = value.astype(BF16)
            hidden_other[i, here, :] = slope.astype(BF16)
        return carry

    def other_backward(m, carry):
        here = span(m)
        ffn_copy(m).wait_recv()
        for i in range(part_chunks):
            grad = dot_nt(ffn_grads_other[here, :], down_w[chunk_span(i), :])
            hidden_other[i, here, :] = (grad * hidden_other[i, here, :].astype(F32)).astype(BF16)
        return carry

    def second_input(m):
        whole, sides, low, high = back_copies(m)
        whole.wait_recv()
        sides.wait_recv()
        pl.when(on_left)(low.wait_recv)
        pl.when(on_right)(high.wait_recv)
        low = conv_back(m, columns_second, WIDE).astype(BF16)
        given[m] = low
        mixed_grads[m] = low.astype(F32)
        grads_across(m).start()

    @pl.when(in_first)
    def _():
        lax.fori_loop(0, rows, other_forward, 0)
        weight_copy.wait_recv()

    pl.when(in_second)(given_load.wait)

    def backward_ffn(m, carry):
        pl.when(in_first)(lambda: second_input(m))
        here = span(m)
        grad = given[m].astype(F32)
        unit = unit_two[here, :].astype(F32)
        grad_ffn = norm_backward(grad * gain_two, unit) * scale_two[here, 0:1]
        sums[1:2, :] += column_sum(grad * unit)
        sums[5:6, :] += column_sum(grad)
        sums[4:5, :] += column_sum(grad_ffn)
        grad_ffn_low = grad_ffn.astype(BF16)
        ffn_grads[here, :] = grad_ffn_low
        ffn_copy(m).start()
        mixed = grad
        for c in range(chunks):
            part = slice(c * width, (c + 1) * width)
            grad_hidden = dot_nt(grad_ffn_low, down_w[part, :]) * slabs[chunks + c, here, :].astype(F32)
            sums[8 + c : 9 + c, :] += column_sum(grad_hidden)
            low = grad_hidden.astype(BF16)
            slabs[chunks + c, here, :] = low
            mixed = mixed + dot_nt(low, up_w[:, part])
        pl.when(in_first)(grads_across(m).wait_send)
        mixed_grads[m] = mixed
        unit = unit_one[here, :].astype(F32)
        grad_conv = norm_backward(mixed * gain_one, unit) * slope_one[here, :].astype(F32)
        sums[0:1, :] += column_sum(mixed * unit)
        sums[3:4, :] += column_sum(mixed)
        sums[2:3, :] += column_sum(grad_conv)
        conv_grads[m, own, :] = grad_conv.astype(BF16)

        @pl.when(in_second)
        def _():
            whole, sides, low, high = back_copies(m)
            pl.when(on_right)(low.start)
            pl.when(on_left)(high.start)
            whole.start()
            sides.start()

        @pl.when(in_first)
        def _():
            low, high = near_copies(m)
            pl.when(on_right)(low.start)
            pl.when(on_left)(high.start)

        half_copy(m).start()
        halves[here, :] = conv_grads[m, own, mine_at]
        return carry

    lax.fori_loop(0, rows, backward_ffn, 0)
    pl.when(in_first)(loads[0].start)

    @pl.when(in_second)
    def _():
        lax.fori_loop(0, rows, other_forward, 0)

    def sums_copy(i):
        return remote(
            sums_sent.at[i], sums_arrived.at[i], sums_send.at[i], sums_recv.at[i], partner(geo.all_bits[i])
        )

    def sums_begin(i):
        sums_sent[i] = sums[...]
        sums_copy(i).start()

    def sums_end(i):
        sums_copy(i).wait_recv()
        sums[...] += sums_arrived[i]

    owners, share = geo.owners, geo.share
    my_bits = {bit: bit_of(bit) for bit in geo.bits}
    partners = {bit: partner(bit) for bit in geo.bits}
    per_dp = geo.seq // geo.low
    first_down, first_conv = part_chunks, 2 * part_chunks

    def columns_of(j):
        single = j == geo.slices - 1 and TAPS % 2 == 1
        return slice(0, half_width) if single else slice(0, width)

    def place(j, owner_dp, owner_seq):
        where = 0
        weight = owners
        for axis, size in geo.orders[j]:
            weight //= 2
            index = owner_dp if axis == "dp" else owner_seq * geo.low
            where = where + ((index // size) % 2 + my_bits[axis, size]) % 2 * weight
        return where

    def part_copy(j, i):
        half, at = owners >> (i + 1), columns_of(j)
        return remote(
            partial.at[j, half : 2 * half, :, at],
            arrived.at[j, half : 2 * half, :, at],
            part_send.at[j, i],
            part_recv.at[j, i],
            partners[geo.orders[j][i]],
        )

    def total_of(j, i):
        half, at = owners >> (i + 1), columns_of(j)
        return partial[j, 0:half, :, at].astype(F32) + arrived[j, half : 2 * half, :, at].astype(F32)

    def advance(j, i):
        part_copy(j, i - 1).wait_recv()
        partial[j, 0 : owners >> i, :, columns_of(j)] = total_of(j, i - 1).astype(BF16)
        part_copy(j, i).start()

    def finish(j):
        last = len(geo.orders[j]) - 1
        part_copy(j, last).wait_recv()
        if j < first_down:
            for part, total in ((my_part, partial[j, 0]), (1 - my_part, arrived[j, 1])):
                at = (part * part_chunks + j) * width
                up_out[:, pl.ds(pl.multiple_of(at, width), width)] = total.astype(F32)
        elif j < first_conv:
            total = total_of(j, last)
            for r in range(2):
                at = (2 * (j - first_down) + r) * share
                down_out[at : at + share, :] = total[r]
        else:
            for q in range(2):
                k = 2 * (j - first_conv) + q
                if k < TAPS:
                    at = slice(q * half_width, (q + 1) * half_width)
                    conv_out[k, :, mine_at] = partial[j, 0, :, at].astype(F32)
                    conv_out[k, :, other_at] = arrived[j, 1, :, at].astype(F32)

    def up_slice(j):
        places = [place(j, owner // per_dp, owner % per_dp) for owner in range(owners)]

        def half(n, carry):
            at = pl.ds(pl.multiple_of(n * half_width, half_width), half_width)
            grad = dot_tn(slabs[2 * chunks], slabs[chunks + chunk_of(j), :, at])
            grad = grad + dot_tn(mixed_other[...], hidden_other[j, :, at])
            for owner in range(owners):
                partial[j, places[owner], :, at] = grad[owner * share : (owner + 1) * share].astype(BF16)
            return carry

        lax.fori_loop(0, 2, half, 0)
        part_copy(j, 0).start()

    def down_slab(i):
        each = owners // chunks
        places = {
            (w, s): place(first_down + s, (chunk_of(i) * each + w) // per_dp, (chunk_of(i) * each + w) % per_dp)
            for w in range(each)
            for s in range(part_chunks)
        }

        def half(n, carry):
            at = pl.ds(pl.multiple_of(n * half_width, half_width), half_width)
            grad = dot_tn(slabs[chunk_of(i)], ffn_grads[:, at])
            grad = grad + dot_tn(upper_other[i], ffn_grads_other[:, at])
            for (w, s), where in places.items():
                for r in range(2):
                    low = ((w * part_chunks + s) * 2 + r) * share
                    partial[first_down + s, where + r, :, at] = grad[low : low + share].astype(BF16)
            return carry

        lax.fori_loop(0, 2, half, 0)
        if i == part_chunks - 1:
            for s in range(part_chunks):
                part_copy(first_down + s, 0).start()

    conv_begun = []

    def conv_slice(p):
        j = first_conv + p
        if not conv_begun:
            conv_begun.append(p)
            for m in range(rows):
                half_copy(m).wait_recv()
            pl.when(in_first)(near_fields.wait_recv)

            @pl.when(in_second)
            def _():
                for m in range(rows):
                    field_copy(m).wait_recv()

        for q in range(2):
            k = 2 * p + q
            if k >= TAPS:
                continue
            at = slice(q * half_width, (q + 1) * half_width)
            places = [place(j, owner // per_dp, owner % per_dp) for owner in range(owners)]
            for flag, dilation in ((in_first, TIGHT), (in_second, WIDE)):

                @pl.when(flag)
                def _(dilation=dilation):
                    def side(chip, carry):
                        grad = None
                        for r in range(rows):
                            m = chip * rows + r
                            term = dot_tn(one_tap(fields, columns, m, k, dilation), halves[span(m), :])
                            grad = term if grad is None else grad + term
                        conv_total[...] = jnp.where(chip == 0, grad, conv_total[...] + grad)
                        return carry

                    lax.fori_loop(0, 2, side, 0)

            for owner in range(owners):
                partial[j, places[owner], :, at] = conv_total[owner * share : (owner + 1) * share].astype(BF16)
        part_copy(j, 0).start()

    input_begun = []

    def first_input(m, carry):
        low, high = near_copies(m)

        @pl.when(on_left)
        def _():
            low.wait_recv()
            conv_grads[m, HALO - EDGE : HALO, :] = near_edges[m, 0]

        @pl.when(on_right)
        def _():
            high.wait_recv()
            conv_grads[m, HALO + length : HALO + length + EDGE, :] = near_edges[m, 1]

        mixed_grads[m] = conv_back(m, columns, TIGHT)
        grads_copy(m).start()
        return carry

    def first_inputs(group):
        if not input_begun:
            input_begun.append(group)
            loads[0].wait()
        each = rows // FIRST_GROUPS
        lax.fori_loop(group * each, (group + 1) * each, first_input, 0)

    def share_sums():
        index = dp * geo.seq + seq
        lane = lax.broadcasted_iota(jnp.int32, (128, width), 1)
        line = lax.broadcasted_iota(jnp.int32, (128, width), 0)
        exact = functools.partial(
            lax.dot_general,
            dimension_numbers=(((1,), (1,)), ((), ())),
            precision=lax.Precision.HIGHEST,
            preferred_element_type=F32,
        )
        picked = exact(sums[...], (lane == line + index * geo.final_share).astype(F32))
        gain_out[...] = picked[0:2, : geo.final_share]
        shift_out[...] = picked[2:6, : geo.final_share]
        start = index * geo.bias_share
        picked = exact(sums[...], (lane == line + start % width).astype(F32))
        wanted = lax.broadcasted_iota(jnp.int32, picked.shape, 0) == 8 + start // width
        bias_out[...] = column_sum(jnp.where(wanted, picked, 0.0))[:, : geo.bias_share]

    def gradients_back():
        lax.fori_loop(0, rows, other_backward, 0)

    def work_of(kind, at):
        if kind == "first":
            return lambda: pl.when(in_first)(lambda: first_inputs(at))
        if kind == "other":
            return gradients_back
        return functools.partial({"up": up_slice, "down": down_slab, "conv": conv_slice}[kind], at)

    sums_begin(0)
    stride = 6
    sums_done = 0
    for at, (what, which) in enumerate(geo.plan):
        if isinstance(what, str):
            work_of(what, which)()
        elif which + 1 < len(geo.orders[what]):
            advance(what, which + 1)
        else:
            finish(what)
        if (at + 1) % stride == 0 and sums_done < len(geo.all_bits):
            sums_end(sums_done)
            sums_done += 1
            if sums_done < len(geo.all_bits):
                sums_begin(sums_done)
            else:
                share_sums()

    for j in range(geo.slices):
        for i in range(len(geo.orders[j])):
            part_copy(j, i).wait_send()
    for i in range(len(geo.all_bits)):
        sums_copy(i).wait_send()
    masks_across.wait_send()

    def settle_row(m, carry):
        act_copy(m).wait()
        half_copy(m).wait_send()
        mixed_copy(m).wait_send()
        ffn_copy(m).wait_send()

        @pl.when(in_first)
        def _():
            grads_copy(m).wait()
            whole, low, high = pass_copies(m)
            pl.when(on_right)(low.wait_send)
            pl.when(on_left)(high.wait_send)
            whole.wait_send()
            low, high = near_copies(m)
            pl.when(on_right)(low.wait_send)
            pl.when(on_left)(high.wait_send)

        @pl.when(in_second)
        def _():
            field_copy(m).wait_send()
            whole, sides, low, high = back_copies(m)
            pl.when(on_right)(low.wait_send)
            pl.when(on_left)(high.wait_send)
            whole.wait_send()
            sides.wait_send()
            grads_across(m).wait_recv()

        return carry

    lax.fori_loop(0, rows, settle_row, 0)

    @pl.when(in_first)
    def _():
        pl.when(on_right)(tokens_right.wait_send)
        pl.when(on_left)(tokens_left.wait_send)
        near_fields.wait_send()

    @pl.when(in_second)
    def _():
        masks_back.wait_send()
        weight_copy.wait_send()


def hand_over(*refs):
    sems_in, sems_out = refs[-2:]
    count = len(refs) // 3
    sources, targets, held = refs[:count], refs[count : 2 * count], refs[2 * count : 3 * count]
    copies_in = [pltpu.make_async_copy(sources[i], held[i], sems_in.at[i]) for i in range(count)]
    copies_out = [pltpu.make_async_copy(held[i], targets[i], sems_out.at[i]) for i in range(count)]
    for copy in copies_in:
        copy.start()
    for i in range(count):
        copies_in[i].wait()
        copies_out[i].start()
    for copy in copies_out:
        copy.wait()


def per_device(
    dp,
    seq,
    tokens,
    cotangent,
    tap_masks,
    conv_weight,
    up_weight,
    up_bias,
    down_weight,
    norm_gains,
    shift_terms,
):
    rows, length, width = tokens.shape
    hidden = up_weight.shape[2]
    geo = Geometry(dp, seq, rows, length, width, hidden)
    reach = length + 2 * HALO
    vmem = pl.BlockSpec(memory_space=pltpu.VMEM)
    hbm = pl.BlockSpec(memory_space=pl.ANY)
    dma = pltpu.SemaphoreType.DMA
    stages = len(geo.all_bits)
    slices = (geo.slices, geo.owners, geo.share, width)
    made = pl.pallas_call(
        functools.partial(body, geo),
        out_shape=[
            jax.ShapeDtypeStruct((rows, length, width), BF16),
            jax.ShapeDtypeStruct((rows, length, width), F32),
            jax.ShapeDtypeStruct((TAPS, geo.share, width), F32),
            jax.ShapeDtypeStruct((geo.share, hidden), F32),
            jax.ShapeDtypeStruct((geo.chunks * geo.share, width), F32),
            jax.ShapeDtypeStruct((1, geo.bias_share), F32),
            jax.ShapeDtypeStruct((2, geo.final_share), F32),
            jax.ShapeDtypeStruct((4, geo.final_share), F32),
        ],
        in_specs=[hbm] * 5 + [vmem] * 4,
        out_specs=[hbm] * 2 + [vmem] * 6,
        scratch_shapes=[
            pltpu.VMEM((2 * rows, reach, width), BF16),
            pltpu.VMEM((rows, reach, width), BF16),
            pltpu.VMEM((rows, 2, EDGE, width), BF16),
            pltpu.VMEM((TAPS * width, width), BF16),
            pltpu.VMEM((width, hidden), BF16),
            pltpu.VMEM((hidden, width), BF16),
            pltpu.VMEM((2 * geo.chunks + 1, geo.tokens, width), BF16),
            pltpu.VMEM((length, TAPS * width), BF16),
            pltpu.VMEM((2 * geo.tokens, width // 2), BF16),
            pltpu.VMEM((geo.tokens, width), BF16),
            pltpu.VMEM((geo.tokens, width), BF16),
            pltpu.VMEM((geo.tokens, width), BF16),
            pltpu.VMEM((geo.tokens, 128), F32),
            pltpu.VMEM((rows, length, width), F32),
            pltpu.VMEM((rows, length, width), BF16),
            pltpu.VMEM((geo.tokens, width), BF16),
            pltpu.VMEM((geo.tokens, width), BF16),
            pltpu.VMEM((geo.tokens, width), BF16),
            pltpu.VMEM((geo.part_chunks, geo.tokens, width), BF16),
            pltpu.VMEM((geo.part_chunks, geo.tokens, width), BF16),
            pltpu.VMEM((rows, length, width), BF16),
            pltpu.VMEM((TAPS, rows, length), jnp.int32),
            pltpu.VMEM((TAPS, rows, length), jnp.int32),
            pltpu.VMEM((2 * geo.tokens, 128), F32),
            pltpu.VMEM((geo.tokens, 128), F32),
            pltpu.VMEM((width, width // 2), F32),
            pltpu.VMEM(slices, BF16),
            pltpu.VMEM(slices, BF16),
            pltpu.VMEM((16, width), F32),
            pltpu.VMEM((stages, 16, width), F32),
            pltpu.VMEM((stages, 16, width), F32),
            dma((3,)),
            dma((2,)),
            dma((2,)),
            dma((2,)),
            dma((2,)),
            dma((2,)),
            dma((rows, 3)),
            dma((rows, 3)),
            dma((rows,)),
            dma((rows,)),
            dma,
            dma,
            dma((rows, 4)),
            dma((rows, 4)),
            dma((rows,)),
            dma((rows,)),
            dma((rows,)),
            dma((rows,)),
            dma((rows,)),
            dma((rows,)),
            dma((rows, 2)),
            dma((rows, 2)),
            dma((rows,)),
            dma((rows,)),
            dma((rows,)),
            dma((rows,)),
            dma((geo.slices, len(geo.bits))),
            dma((geo.slices, len(geo.bits))),
            dma((stages,)),
            dma((stages,)),
        ],
        compiler_params=pltpu.CompilerParams(
            collective_id=0, has_side_effects=True, vmem_limit_bytes=63 * 2**20
        ),
    )(
        tokens,
        cotangent,
        jnp.transpose(conv_weight[0], (1, 0, 2)).reshape(TAPS * width, width),
        up_weight[0],
        down_weight[0],
        tap_masks[0],
        up_bias,
        jnp.transpose(norm_gains[0]),
        jnp.transpose(shift_terms[0]),
    )
    made = pl.pallas_call(
        hand_over,
        out_shape=[jax.ShapeDtypeStruct(array.shape, array.dtype) for array in made],
        in_specs=[hbm] * len(made),
        out_specs=[hbm] * len(made),
        scratch_shapes=[pltpu.VMEM(array.shape, array.dtype) for array in made] + [dma((len(made),))] * 2,
    )(*made)
    act, grads, conv_grad, up_grad, down_grad, bias_grad, gain_grad, shift_grad = made
    conv_grad = jnp.transpose(conv_grad, (1, 0, 2))
    if geo.low > 1:
        groups = [list(range(at, at + geo.low)) for at in range(0, seq, geo.low)]
        conv_grad, up_grad, down_grad = (
            lax.psum_scatter(
                grad, "seq", scatter_dimension=0, axis_index_groups=groups, tiled=True
            )
            for grad in (conv_grad, up_grad, down_grad)
        )
    return (
        act[None],
        grads[None],
        conv_grad[None],
        up_grad[None],
        bias_grad,
        down_grad[None],
        jnp.transpose(gain_grad)[None],
        jnp.transpose(shift_grad)[None],
    )


def solution(mesh):
    placed = (
        P("dp", "seq", None),
        P("dp", "seq", None),
        P("section", None, "dp", "seq"),
        P("section", None, None, None),
        P("section", None, None),
        P("section", None),
        P("section", None, None),
        P("section", None, None),
        P("section", None, None),
    )
    return jax.shard_map(
        functools.partial(per_device, mesh.shape["dp"], mesh.shape["seq"]),
        mesh=mesh,
        in_specs=placed,
        out_specs=(
            P("section", "dp", "seq", None),
            P("section", "dp", "seq", None),
            P("section", ("dp", "seq"), None, None),
            P("section", ("dp", "seq"), None),
            P("section", ("dp", "seq")),
            P("section", ("dp", "seq"), None),
            P("section", ("dp", "seq"), None),
            P("section", ("dp", "seq"), None),
        ),
        check_vma=False,
    )
```

profile of v0, /device:TPU:0, one launch (start us, length us, event | category | flops | bytes accessed | tf_op | source)
XLA Modules:
  0.0 117.2 jit_solution(14160644581031202381)
XLA Ops:
  0.6 112.6 %shard_map.152 = (bf16[4,256,512]{2,1,0:T(8,128)(2,1)}, f32[4,256,512]{2,1,0:T(8,128)}, f32[9,32,512]{2,1,0:T(8,128)}, f32[32,2048]{1,0:T(8,128)}, f32[128,512]{...) custom-call(bf16[4,256,512]{2,1,0:T(8,128)(2,1)} %tokens_hbm.1, ...), custom_call_target="tpu_custom_call" | custom-call | tf_op jit(solution)/shard_map/pallas_call | solution.py:907
  113.3 3.7 %shard_map.153 = (bf16[4,256,512]{2,1,0:T(8,128)(2,1)}, f32[4,256,512]{2,1,0:T(8,128)}, f32[9,32,512]{2,1,0:T(8,128)}, f32[32,2048]{1,0:T(8,128)}, f32[128,512]{...) custom-call(bf16[4,256,512]{2,1,0:T(8,128)(2,1)} %get-tuple-element.24.refs_0_, ...), custom_call_target="tpu_custom_call" | custom-call | tf_op jit(solution)/shard_map/pallas_call | solution.py:998
where the time goes:
time: 117 us
  Pallas kernels  116 us (99%)
    pallas_call x1, Pallas kernels, per_device(): pl.pallas_call(functools.partial(body, geo), out_shape=[jax.ShapeDtypeStr...  113 us
    pallas_call x1, Pallas kernels, per_device(): pl.pallas_call(hand_over, out_shape=[jax.ShapeDtypeStruct(array.shape, ar...  3.74 us

commit v1 on v0

--- a/solution.py
+++ b/solution.py
@@ -20,9 +20,9 @@
 LAG = 3
 FIRST_GROUPS = 2
 PLAN = (
-    ("conv", 4), ("conv", 3), ("conv", 1), (8, 0), ("other", 0), ("up", 1), (7, 0), (8, 1), ("conv", 0), (5, 0),
-    ("first", 0), ("conv", 2), ("down", 0), (8, 2), ("up", 0), (4, 0), (7, 1), ("down", 1), (1, 0), (0, 0), (4, 1),
-    (6, 0), (7, 2), (5, 1), (2, 0), (1, 1), (3, 0), (6, 1), (5, 2), (0, 1), ("first", 1), (5, 3), (7, 3), (4, 2),
+    ("first", 0), ("conv", 4), ("conv", 3), ("conv", 1), (8, 0), ("other", 0), ("up", 1), (7, 0), ("first", 1),
+    (8, 1), ("conv", 0), (5, 0), ("conv", 2), ("down", 0), (8, 2), ("up", 0), (4, 0), (7, 1), ("down", 1), (1, 0),
+    (0, 0), (4, 1), (6, 0), (7, 2), (5, 1), (2, 0), (1, 1), (3, 0), (6, 1), (5, 2), (0, 1), (5, 3), (7, 3), (4, 2),
     (3, 1), (2, 1), (6, 2), (1, 2), (8, 3), (0, 2), (3, 2), (6, 3), (4, 3), (1, 3), (0, 3), (2, 2),
 )
 ALONG = (5, 7, 8)
@@ -253,6 +253,21 @@
         load.start()
     pl.when(in_second)(given_load.start)
 
+    barrier = pltpu.get_barrier_semaphore()
+
+    def greet(device):
+        pl.semaphore_signal(barrier, inc=1, device_id=device, device_id_type=MESH)
+
+    for bit in geo.all_bits:
+        greet(partner(bit))
+    greet(core)
+    for flag, at in ((on_left, seq - 1), (on_right, seq + 1)):
+
+        @pl.when(flag)
+        def _(at=at):
+            greet((section, dp, at))
+            greet((1 - section, dp, at))
+
     @pl.when(has_left == 0)
     def _():
         fields[0:rows, :HALO] = jnp.zeros((rows, HALO, width), BF16)
@@ -264,22 +279,6 @@
         conv_grads[:, HALO + length :] = jnp.zeros((rows, HALO, width), BF16)
 
     sums[...] = jnp.zeros(sums.shape, F32)
-
-    barrier = pltpu.get_barrier_semaphore()
-
-    def greet(device):
-        pl.semaphore_signal(barrier, inc=1, device_id=device, device_id_type=MESH)
-
-    for bit in geo.all_bits:
-        greet(partner(bit))
-    greet(core)
-    for flag, at in ((on_left, seq - 1), (on_right, seq + 1)):
-
-        @pl.when(flag)
-        def _(at=at):
-            greet((section, dp, at))
-            greet((1 - section, dp, at))
-
     pl.semaphore_wait(barrier, len(geo.all_bits) + 1 + 2 * has_left + 2 * has_right)
 
     tokens_right = remote(
@@ -544,7 +543,11 @@
     pl.when(in_second)(given_load.wait)
 
     def backward_ffn(m, carry):
-        pl.when(in_first)(lambda: second_input(m))
+        @pl.when(in_first)
+        def _():
+            second_input(m)
+            pl.when(m == rows - 1)(loads[0].start)
+
         here = span(m)
         grad = given[m].astype(F32)
         unit = unit_two[here, :].astype(F32)
@@ -591,7 +594,6 @@
         return carry
 
     lax.fori_loop(0, rows, backward_ffn, 0)
-    pl.when(in_first)(loads[0].start)
 
     @pl.when(in_second)
     def _():

time: 117 us -> 117 us (level)
  no operation moved by 1% of the time
where the time goes in v1:
time: 117 us; the launch traced here: 116 us
  Pallas kernels  116 us (99%)
    pallas_call x1, Pallas kernels, per_device(): pl.pallas_call(functools.partial(body, geo), out_shape=[jax.ShapeDtypeStr...  112 us
    pallas_call x1, Pallas kernels, per_device(): pl.pallas_call(hand_over, out_shape=[jax.ShapeDtypeStruct(array.shape, ar...  3.74 us

profile of v1, /device:TPU:0, one launch (start us, length us, event | category | flops | bytes accessed | tf_op | source)
XLA Modules:
  0.0 116.4 jit_solution(381512533524189338)
XLA Ops:
  0.6 111.8 %shard_map.152 = (bf16[4,256,512]{2,1,0:T(8,128)(2,1)}, f32[4,256,512]{2,1,0:T(8,128)}, f32[9,32,512]{2,1,0:T(8,128)}, f32[32,2048]{1,0:T(8,128)}, f32[128,512]{...) custom-call(bf16[4,256,512]{2,1,0:T(8,128)(2,1)} %tokens_hbm.1, ...), custom_call_target="tpu_custom_call" | custom-call | tf_op jit(solution)/shard_map/pallas_call | solution.py:909
  112.5 3.7 %shard_map.153 = (bf16[4,256,512]{2,1,0:T(8,128)(2,1)}, f32[4,256,512]{2,1,0:T(8,128)}, f32[9,32,512]{2,1,0:T(8,128)}, f32[32,2048]{1,0:T(8,128)}, f32[128,512]{...) custom-call(bf16[4,256,512]{2,1,0:T(8,128)(2,1)} %get-tuple-element.24.refs_0_, ...), custom_call_target="tpu_custom_call" | custom-call | tf_op jit(solution)/shard_map/pallas_call | solution.py:1000

commit v2 on v1

--- a/solution.py
+++ b/solution.py
@@ -20,12 +20,12 @@
 LAG = 3
 FIRST_GROUPS = 2
 PLAN = (
-    ("first", 0), ("conv", 4), ("conv", 3), ("conv", 1), (8, 0), ("other", 0), ("up", 1), (7, 0), ("first", 1),
-    (8, 1), ("conv", 0), (5, 0), ("conv", 2), ("down", 0), (8, 2), ("up", 0), (4, 0), (7, 1), ("down", 1), (1, 0),
-    (0, 0), (4, 1), (6, 0), (7, 2), (5, 1), (2, 0), (1, 1), (3, 0), (6, 1), (5, 2), (0, 1), (5, 3), (7, 3), (4, 2),
-    (3, 1), (2, 1), (6, 2), (1, 2), (8, 3), (0, 2), (3, 2), (6, 3), (4, 3), (1, 3), (0, 3), (2, 2),
+    ("first", 0), ("conv", 4), ("conv", 0), ("other", 0), (8, 0), ("up", 1), ("up", 0), (8, 1), ("first", 1),
+    ("conv", 2), (4, 0), ("conv", 3), (0, 0), ("conv", 1), (6, 0), (0, 1), ("down", 0), (1, 0), (4, 1), (8, 2),
+    (7, 0), (6, 1), ("down", 1), (1, 1), (7, 1), (5, 0), (2, 0), (6, 2), (6, 3), (3, 0), (1, 2), (0, 2), (5, 1),
+    (4, 2), (7, 2), (0, 3), (2, 1), (3, 1), (4, 3), (8, 3), (5, 2), (7, 3), (2, 2), (1, 3), (5, 3), (3, 2),
 )
-ALONG = (5, 7, 8)
+ALONG = (1, 4, 8)
 TANH_SCALE = 0.7978845608028654
 TANH_CUBE = TANH_SCALE * 0.044715
 

time: 117 us -> 118 us (level)
    pallas_call x1, Pallas kernels: 112 us -> 114 us  [per_device(): pl.pallas_call(functools.partial(body, geo), out_shape=[jax.ShapeDtypeStr...]
where the time goes in v2:
time: 118 us
  Pallas kernels  117 us (99%)
    pallas_call x1, Pallas kernels, per_device(): pl.pallas_call(functools.partial(body, geo), out_shape=[jax.ShapeDtypeStr...  114 us
    pallas_call x1, Pallas kernels, per_device(): pl.pallas_call(hand_over, out_shape=[jax.ShapeDtypeStruct(array.shape, ar...  3.74 us

profile of v2, /device:TPU:0, one launch (start us, length us, event | category | flops | bytes accessed | tf_op | source)
XLA Modules:
  0.0 118.3 jit_solution(8882062886896150290)
XLA Ops:
  0.6 113.7 %shard_map.152 = (bf16[4,256,512]{2,1,0:T(8,128)(2,1)}, f32[4,256,512]{2,1,0:T(8,128)}, f32[9,32,512]{2,1,0:T(8,128)}, f32[32,2048]{1,0:T(8,128)}, f32[128,512]{...) custom-call(bf16[4,256,512]{2,1,0:T(8,128)(2,1)} %tokens_hbm.1, ...), custom_call_target="tpu_custom_call" | custom-call | tf_op jit(solution)/shard_map/pallas_call | solution.py:909
  114.3 3.7 %shard_map.153 = (bf16[4,256,512]{2,1,0:T(8,128)(2,1)}, f32[4,256,512]{2,1,0:T(8,128)}, f32[9,32,512]{2,1,0:T(8,128)}, f32[32,2048]{1,0:T(8,128)}, f32[128,512]{...) custom-call(bf16[4,256,512]{2,1,0:T(8,128)(2,1)} %get-tuple-element.24.refs_0_, ...), custom_call_target="tpu_custom_call" | custom-call | tf_op jit(solution)/shard_map/pallas_call | solution.py:1000
